TPU v7x, 32 devices: a whole 2x2x4 slice. The times are simulated.
32 devices in a mesh: row: 2 (over y), col: 16 (over z, x, core).
Axes of the slice: x: 2, y: 2, z: 4, core: 2. Of those that a mesh axis runs over, the one named last changes fastest.
Arguments:
- inputs: bfloat16 [512, 9216], P('col', 'row'), may hold values from -6 to 6
- out_grad: bfloat16 [512, 9216], P('col', 'row'), may hold values from -6 to 6
- preact: bfloat16 [512, 36864], P('row', 'col'), may hold values from -6 to 6
- first_weight: bfloat16 [9216, 36864], P('row', 'col'), may hold values from -0.0625 to 0.0625
- second_weight: bfloat16 [36864, 9216], P('col', 'row'), may hold values from -0.03125 to 0.03125
Outputs:
- grad_inputs: float32 [512, 9216], P('col', 'row')
- grad_first: bfloat16 [9216, 36864], P('row', 'col')
- grad_second: bfloat16 [36864, 9216], P('col', 'row')
All inputs are finite; a program needn't handle non-finite values.
Results may differ from a plain program's by a relative error of at most 0.005.
Values may be sent and summed in bfloat16 or wider, within the bound.
A program may use at most 192 MiB of HBM per device.

v0:
```python
import math

import jax
import jax.numpy as jnp
from jax import lax
from jax.sharding import PartitionSpec as P

INV_ROOT_TWO = 0.7071067811865476
INV_ROOT_TWO_PI = 0.3989422804014327


def gelu_value(values):
    return 0.5 * values * (1.0 + lax.erf(values * INV_ROOT_TWO))


def gelu_slope(values):
    normal_cdf = 0.5 * (1.0 + lax.erf(values * INV_ROOT_TWO))
    density = jnp.exp(-0.5 * values * values) * INV_ROOT_TWO_PI
    return normal_cdf + values * density


def contract_rows(left, right):
    return lax.dot_general(
        left, right, (((0,), (0,)), ((), ())), preferred_element_type=jnp.float32
    )


def contract_cols(left, right):
    return lax.dot_general(
        left, right, (((1,), (1,)), ((), ())), preferred_element_type=jnp.float32
    )


def on_device(inputs, out_grad, preact, first_weight, second_weight):
    pre_rows = lax.all_gather(preact, "row", axis=0, tiled=True)
    pre_whole = pre_rows.astype(jnp.float32)
    activated = gelu_value(pre_whole).astype(jnp.bfloat16)
    input_whole, grad_whole = (
        lax.all_gather(inputs, "col", axis=0, tiled=True),
        lax.all_gather(out_grad, "col", axis=0, tiled=True),
    )
    tokens_all = grad_whole.shape[0]
    factor = 1.0 / math.sqrt(tokens_all)
    token_rows = grad_whole
    grad_act = lax.psum_scatter(
        contract_cols(token_rows, second_weight), "row", scatter_dimension=0, tiled=True
    )
    grad_own = (grad_act * gelu_slope(preact.astype(jnp.float32))).astype(jnp.bfloat16)
    grad_pre = lax.all_gather(grad_own, "row", axis=0, tiled=True)
    grad_second = (contract_rows(activated, grad_whole) * factor).astype(jnp.bfloat16)
    first_total = contract_rows(input_whole, grad_pre)
    grad_first = (first_total * factor).astype(jnp.bfloat16)
    token_rows = grad_pre
    grad_inputs = lax.psum_scatter(
        contract_cols(token_rows, first_weight), "col", scatter_dimension=0, tiled=True
    )
    return (grad_inputs, grad_first, grad_second)


def solution(mesh):
    placed = (P("col", "row"), P("col", "row"), P("row", "col"), P("row", "col"), P("col", "row"))
    return jax.shard_map(
        on_device,
        mesh=mesh,
        in_specs=placed,
        out_specs=(P("col", "row"), P("row", "col"), P("col", "row")),
        check_vma=False,
    )
```

profile of v0, /device:TPU:0, one launch (start us, length us, event | category | flops | bytes accessed | tf_op | source)
XLA Modules:
  0.0 396.5 jit_solution(9279631531955513067)
XLA Ops:
  7.2 0.0 all-gather.5.cloned.1.call-start
  7.2 0.7 all-gather.5.cloned.1.call-update
  7.9 0.0 reduce-scatter.3.cloned.1.call-start
  7.9 58.3 %all-gather.5.cloned.1.call-done = bf16[512,4608]{1,0:T(8,128)(2,1)} async-done(((bf16[32,4608]{1,0:T(8,128)(2,1)}), bf16[512,4608]{1,0:T(8,128)(2,1)}) %all-gather.5.cloned.1.call-update) | async-done | bytes 4718608 | tf_op jit(solution)/shard_map/all_gather | solution.py:40
  66.2 17.1 %fusion.20 = f32[512,2304]{1,0:T(8,128)} fusion(bf16[512,4608]{1,0:T(8,128)(2,1)} %all-gather.5.cloned.1.call-done, bf16[2304,4608]{1,0:T(8,128)(2,1)} %param.9), kind=kOutput, calls=%fused_computation.27 | convolution fusion | flops 10871635968 | bytes 30670848 | tf_op jit(solution)/shard_map/dot_general | solution.py:29
  83.3 0.0 copy-start
  83.3 0.0 reduce-scatter.3.cloned.1.call-update
  83.3 0.0 all-gather.7.cloned.1.call-start
  83.4 58.7 %reduce-scatter.3.cloned.1.call-done = f32[256,2304]{1,0:T(8,128)} async-done(((f32[512,2304]{1,0:T(8,128)}), f32[256,2304]{1,0:T(8,128)}) %reduce-scatter.3.cloned.1.call-update) | async-done | bytes 2359312 | tf_op jit(solution)/shard_map/reduce_scatter | solution.py:45
  142.0 0.0 copy-done
  142.0 3.1 fusion.16
  145.2 0.0 all-gather.7.cloned.1.call-update
  145.2 0.0 all-gather.11.cloned.1.call-start
  145.2 0.5 all-gather.11.cloned.1.call-update
  145.8 0.0 all-gather.9.cloned.1.call-start
  145.8 0.5 all-gather.9.cloned.1.call-update
  146.4 0.2 reduce-scatter.5.cloned.1.call-start
  146.6 34.8 %all-gather.7.cloned.1.call-done = bf16[512,2304]{1,0:T(8,128)(2,1)} async-done(((bf16[256,2304]{1,0:T(8,128)(2,1)}), bf16[512,2304]{1,0:T(8,128)(2,1)}) %all-gather.7.cloned.1.call-update) | async-done | bytes 2359312 | tf_op jit(solution)/shard_map/all_gather | solution.py:49
  181.4 18.2 %fusion.21 = f32[512,4608]{1,0:T(8,128)} fusion(bf16[512,2304]{1,0:T(8,128)(2,1)} %all-gather.7.cloned.1.call-done, bf16[4608,2304]{1,0:T(8,128)(2,1)} %param.8), kind=kOutput, calls=%fused_computation.28 | convolution fusion | flops 10871635968 | bytes 33030144 | tf_op jit(solution)/shard_map/dot_general | solution.py:29
  199.6 0.0 reduce-scatter.5.cloned.1.call-update
  199.6 0.0 copy-start.1
  199.6 19.3 %all-gather.11.cloned.1.call-done = bf16[512,2304]{1,0:T(8,128)(2,1)} async-done(((bf16[256,2304]{1,0:T(8,128)(2,1)}), bf16[512,2304]{1,0:T(8,128)(2,1)}) %all-gather.11.cloned.1.call-update) | async-done | bytes 2359312 | tf_op jit(solution)/shard_map/all_gather | solution.py:35
  219.0 18.4 %multiply_convert_fusion = bf16[2304,4608]{1,0:T(8,128)(2,1)} fusion(bf16[512,4608]{1,0:T(8,128)(2,1)} %all-gather.5.cloned.1.call-done, bf16[512,2304]{1,0:T(8,128)(2,1)} %all-gather.11.cloned.1.call-done), kind=kOutput, calls=%fused_computation | convolution fusion | flops 10899947520 | bytes 28311552 | tf_op jit(solution)/shard_map/dot_general | solution.py:23
  237.4 37.3 %all-gather.9.cloned.1.call-done = bf16[512,4608]{1,0:T(8,128)(2,1)} async-done(((bf16[32,4608]{1,0:T(8,128)(2,1)}), bf16[512,4608]{1,0:T(8,128)(2,1)}) %all-gather.9.cloned.1.call-update) | async-done | bytes 4718608 | tf_op jit(solution)/shard_map/all_gather | solution.py:39
  274.6 0.0 copy-done.1
  274.6 17.2 %fusion = bf16[4608,2304]{0,1:T(8,128)(2,1)} fusion(bf16[512,2304]{1,0:T(8,128)(2,1)S(1)} %copy-done.1, bf16[512,4608]{1,0:T(8,128)(2,1)} %all-gather.9.cloned.1.call-done), kind=kOutput, calls=%fused_computation.2 | convolution fusion | flops 10892869632 | bytes 28311552 | tf_op jit(solution)/shard_map/dot_general | solution.py:23
  291.9 27.8 %copy.8 = bf16[4608,2304]{1,0:T(8,128)(2,1)} copy(bf16[4608,2304]{0,1:T(8,128)(2,1)} %fusion) | data formatting | bytes 42467328
  319.7 70.0 %reduce-scatter.5.cloned.1.call-done = f32[32,4608]{1,0:T(8,128)} async-done(((f32[512,4608]{1,0:T(8,128)}), f32[32,4608]{1,0:T(8,128)}) %reduce-scatter.5.cloned.1.call-update) | async-done | bytes 589840 | tf_op jit(solution)/shard_map/reduce_scatter | solution.py:54
Async XLA Ops:
  7.2 59.1 %all-gather.5.cloned.1.call-start = ((), (), s32[]{:S(2)}) async-start(), calls=%async_computation.2 | async-start | bytes 5013504 | tf_op jit(solution)/shard_map/all_gather | solution.py:40
  7.9 134.1 %reduce-scatter.3.cloned.1.call-start = ((), (), s32[]{:S(2)}) async-start(), calls=%async_computation.3 | async-start | bytes 7077888 | tf_op jit(solution)/shard_map/reduce_scatter | solution.py:45
  83.3 58.7 %copy-start = (bf16[256,2304]{1,0:T(8,128)(2,1)S(1)}, bf16[256,2304]{1,0:T(8,128)(2,1)}, u32[]{:S(2)}) copy-start(bf16[256,2304]{1,0:T(8,128)(2,1)} %param.7) | copy-start | bytes 3538948
  83.3 98.1 %all-gather.7.cloned.1.call-start = ((), (), s32[]{:S(2)}) async-start(), calls=%async_computation.4 | async-start | bytes 3538944 | tf_op jit(solution)/shard_map/all_gather | solution.py:49
  145.2 73.8 %all-gather.11.cloned.1.call-start = ((), (), s32[]{:S(2)}) async-start(), calls=%async_computation.7 | async-start | bytes 3538944 | tf_op jit(solution)/shard_map/all_gather | solution.py:35
  145.8 128.9 %all-gather.9.cloned.1.call-start = ((), (), s32[]{:S(2)}) async-start(), calls=%async_computation.6 | async-start | bytes 5013504 | tf_op jit(solution)/shard_map/all_gather | solution.py:39
  146.4 243.3 %reduce-scatter.5.cloned.1.call-start = ((), (), s32[]{:S(2)}) async-start(), calls=%async_computation.5 | async-start | bytes 10027008 | tf_op jit(solution)/shard_map/reduce_scatter | solution.py:54
  199.6 75.0 %copy-start.1 = (bf16[512,2304]{1,0:T(8,128)(2,1)S(1)}, bf16[512,2304]{1,0:T(8,128)(2,1)}, u32[]{:S(2)}) copy-start(bf16[512,2304]{1,0:T(8,128)(2,1)} %all-gather.7.cloned.1.call-done) | copy-start | bytes 7077892
Sparse Core Ops, SparseCore 0:
  10.3 55.9 all-gather.4
  83.4 58.5 reduce-scatter.2
  145.3 36.0 all-gather.6
  182.9 36.0 all-gather.10
  221.4 53.2 all-gather.8
  279.7 109.9 reduce-scatter.4
where the time goes:
time: 397 us
  waiting for transfers between devices  280 us (71%)
  matrix products  70.8 us (18%)
  local copies, waits for them, and re-layouts  27.8 us (7%)
  between operations  14.1 us (4%)
    reduce_scatter x1, waiting for transfers between devices, on_device(): lax.psum_scatter(contract_cols(token_rows, first_weight), 'col', scatter_...  70 us
    reduce_scatter x1, waiting for transfers between devices, on_device(): lax.psum_scatter(contract_cols(token_rows, second_weight), 'row', scatter...  58.7 us
    all_gather x1, waiting for transfers between devices, on_device(): lax.all_gather(out_grad, 'col', axis=0, tiled=True)  58.3 us
    all_gather x1, waiting for transfers between devices, on_device(): lax.all_gather(inputs, 'col', axis=0, tiled=True)  37.3 us
    dot_general x2, matrix products, contract_rows(): lax.dot_general(left, right, (((0,), (0,)), ((), ())), preferred_element_...  35.6 us
    dot_general x2, matrix products, contract_cols(): lax.dot_general(left, right, (((1,), (1,)), ((), ())), preferred_element_...  35.2 us
    all_gather x1, waiting for transfers between devices, on_device(): grad_pre = lax.all_gather(grad_own, 'row', axis=0, tiled=True)  34.8 us
    unnamed x5, local copies, waits for them, and re-layouts  27.8 us
  transfers between devices with their start and end apart: 6, of which 6 were waited for; matrix products, arithmetic and copies ran while one was open for 21% of the time, Pallas kernels for 0%

commit v1 on v0

v1 whole, which is shorter than its diff:
```python
import functools
import math

import jax
import jax.numpy as jnp
from jax import lax
from jax.experimental import pallas as pl
from jax.experimental.pallas import tpu as pltpu
from jax.sharding import PartitionSpec as P

INV_ROOT_TWO = 0.7071067811865476
INV_ROOT_TWO_PI = 0.3989422804014327
MESH = pl.DeviceIdType.MESH
VMEM_LIMIT = 58 * 1024 * 1024


def gelu_value(values):
    return 0.5 * values * (1.0 + lax.erf(values * INV_ROOT_TWO))


def gelu_slope(values):
    normal_cdf = 0.5 * (1.0 + lax.erf(values * INV_ROOT_TWO))
    density = jnp.exp(-0.5 * values * values) * INV_ROOT_TWO_PI
    return normal_cdf + values * density


def contract_rows(left, right):
    return lax.dot_general(
        left, right, (((0,), (0,)), ((), ())), preferred_element_type=jnp.float32
    )


def contract_cols(left, right):
    return lax.dot_general(
        left, right, (((1,), (1,)), ((), ())), preferred_element_type=jnp.float32
    )


def tile_of(size):
    return next(t for t in (256, 384, 128, size) if size % t == 0)


def cut_of(width):
    return width // 256 * 128


def ring_position(chip, chips):
    odd = lax.rem(chip, 2)
    half = lax.div(chip, 2)
    return half + odd * (chips - 1 - 2 * half)


def ring_chip(position, chips):
    evens = (chips + 1) // 2
    position = lax.rem(position + 2 * chips, chips)
    upper = (position >= evens).astype(jnp.int32)
    return 2 * position + upper * (2 * (chips - 1 - position) + 1 - 2 * position)


def enter(col_peers, row_size, row):
    barrier = pltpu.get_barrier_semaphore()
    for peer in col_peers:
        pl.semaphore_signal(barrier, inc=1, device_id={"col": peer}, device_id_type=MESH)
    for shift in range(1, row_size):
        pl.semaphore_signal(
            barrier, inc=1, device_id={"row": lax.rem(row + shift, row_size)}, device_id_type=MESH
        )
    pl.semaphore_wait(barrier, len(col_peers) + row_size - 1)


def gather_kernel(
    row_size, chips, grad_ref, pre_ref, weight_ref,
    full_ref, pre_full_ref, sum_ref, low_ref,
    weight, rows, out_sum, out_low,
    weight_sem, local_sem, side_send, side_recv, pre_send, pre_recv,
    right_send, right_recv, left_send, left_recv, store_sem,
):
    row, col = lax.axis_index("row"), lax.axis_index("col")
    chip, core = lax.div(col, 2), lax.rem(col, 2)
    place = ring_position(chip, chips)
    at = lambda delta: 2 * ring_chip(place + delta, chips) + core
    right, left, side = at(1), at(-1), 2 * chip + 1 - core
    half = chips // 2
    tile = tile_of(weight.shape[0])
    tiles = weight.shape[0] // tile
    block = grad_ref.shape[0]
    width = grad_ref.shape[1]
    cut = cut_of(width)

    def weight_copy(j):
        piece = pl.ds(j * tile, tile)
        return pltpu.make_async_copy(weight_ref.at[piece], weight.at[piece], weight_sem.at[j])

    own = pltpu.make_async_copy(grad_ref, full_ref.at[col], local_sem.at[0])
    own.start()
    for j in range(tiles):
        weight_copy(j).start()
    pre_own = pltpu.make_async_copy(pre_ref, pre_full_ref.at[row], local_sem.at[1])
    pre_own.start()
    enter((right, left, side), row_size, row)
    own.wait()

    def to_col(index, lo, size, peer, send, recv):
        piece = full_ref.at[index, :, pl.ds(lo, size)]
        return pltpu.make_async_remote_copy(
            src_ref=piece, dst_ref=piece, send_sem=send, recv_sem=recv,
            device_id={"col": peer}, device_id_type=MESH,
        )

    def go_right(step):
        size = cut if step == half else width
        return to_col(at(1 - step), 0, size, right, right_send.at[step - 1], right_recv.at[step - 1])

    def go_left(step):
        lo, size = (cut, width - cut) if step == half else (0, width)
        return to_col(at(step - 1), lo, size, left, left_send.at[step - 1], left_recv.at[step - 1])

    def from_left(step):
        size = cut if step == half else width
        return to_col(at(-step), 0, size, right, right_send.at[step - 1], right_recv.at[step - 1])

    def from_right(step):
        lo, size = (cut, width - cut) if step == half else (0, width)
        return to_col(at(step), lo, size, left, left_send.at[step - 1], left_recv.at[step - 1])

    def sideways(delta, mine, slot):
        index = at(delta)
        if not mine:
            index = index + 1 - 2 * core
        return to_col(index, 0, width, side, side_send.at[slot], side_recv.at[slot])

    go_right(1).start()
    go_left(1).start()
    sideways(0, True, 0).start()
    pre_copies = []
    for shift in range(1, row_size):
        pre_copies.append(pltpu.make_async_remote_copy(
            src_ref=pre_ref, dst_ref=pre_full_ref.at[row],
            send_sem=pre_send.at[shift - 1], recv_sem=pre_recv.at[shift - 1],
            device_id={"row": lax.rem(row + shift, row_size)}, device_id_type=MESH,
        ))
        pre_copies[-1].start()

    def multiply(deltas, first):
        count = 2 * block * len(deltas)
        for i, delta in enumerate(deltas):
            origin = 2 * ring_chip(place + delta, chips)
            for k in range(2):
                rows[pl.ds((2 * i + k) * block, block), :] = full_ref[origin + k]

        @pl.loop(0, tiles)
        def _(j):
            piece = pl.ds(pl.multiple_of(j * tile, tile), tile)
            if first:
                pltpu.make_async_copy(
                    weight_ref.at[piece], weight.at[piece], weight_sem.at[j]
                ).wait()
            part = contract_cols(rows[pl.ds(0, count), :], weight[piece, :])
            low = part.astype(jnp.bfloat16)
            for i, delta in enumerate(deltas):
                origin = pl.multiple_of(2 * block * ring_chip(place + delta, chips), 2 * block)
                out_sum[pl.ds(origin, 2 * block), piece] = part[2 * block * i:2 * block * (i + 1)]
                out_low[pl.ds(origin, 2 * block), piece] = low[2 * block * i:2 * block * (i + 1)]

    slot = 1
    sideways(0, False, 0).wait_recv()
    for step in range(1, half + 1):
        deltas = (0,) if step == 1 else (step - 1, 1 - step)
        multiply(deltas, step == 1)
        from_left(step).wait_recv()
        if step < half:
            go_right(step + 1).start()
        from_right(step).wait_recv()
        if step < half:
            go_left(step + 1).start()
        moved = (half,) if step == half else (step, -step)
        for i, delta in enumerate(moved):
            sideways(delta, True, slot + i).start()
        for i, delta in enumerate(moved):
            sideways(delta, False, slot + i).wait_recv()
        slot += len(moved)
    multiply((half,), False)

    out_copies = [
        pltpu.make_async_copy(out_sum, sum_ref, store_sem.at[0]),
        pltpu.make_async_copy(out_low, low_ref, store_sem.at[1]),
    ]
    for copy in out_copies:
        copy.start()
    for step in range(1, half + 1):
        go_right(step).wait_send()
        go_left(step).wait_send()
    slot = 0
    for step in range(0, half + 1):
        moved = (step,) if step in (0, half) else (step, -step)
        for i, delta in enumerate(moved):
            sideways(delta, True, slot + i).wait_send()
        slot += len(moved)
    pre_own.wait()
    for shift in range(1, row_size):
        pre_copies[shift - 1].wait_send()
        source = lax.rem(row + row_size - shift, row_size)
        pltpu.make_async_remote_copy(
            src_ref=pre_ref, dst_ref=pre_full_ref.at[source],
            send_sem=pre_send.at[shift - 1], recv_sem=pre_recv.at[shift - 1],
            device_id={"row": lax.rem(row + shift, row_size)}, device_id_type=MESH,
        ).wait_recv()
    for copy in out_copies:
        copy.wait()


def gather_and_multiply(row_size, col_size, out_grad, preact, weight):
    chips, half = col_size // 2, col_size // 4
    block, width = out_grad.shape
    tokens, hidden = block * col_size, weight.shape[0]
    dma = pltpu.SemaphoreType.DMA
    anywhere = pl.BlockSpec(memory_space=pl.ANY)
    vmem = pl.BlockSpec(memory_space=pltpu.VMEM)
    flops = 2 * tokens * hidden * width
    return pl.pallas_call(
        functools.partial(gather_kernel, row_size, chips),
        out_shape=(
            jax.ShapeDtypeStruct((col_size, block, width), jnp.bfloat16),
            jax.ShapeDtypeStruct((row_size,) + preact.shape, jnp.bfloat16),
            jax.ShapeDtypeStruct((tokens, hidden), jnp.float32),
            jax.ShapeDtypeStruct((tokens, hidden), jnp.bfloat16),
        ),
        in_specs=[anywhere] * 3,
        out_specs=(vmem, anywhere, anywhere, anywhere),
        scratch_shapes=[
            pltpu.VMEM(weight.shape, jnp.bfloat16),
            pltpu.VMEM((4 * block, width), jnp.bfloat16),
            pltpu.VMEM((tokens, hidden), jnp.float32),
            pltpu.VMEM((tokens, hidden), jnp.bfloat16),
            dma((hidden // tile_of(hidden),)), dma((2,)), dma((chips,)), dma((chips,)),
            dma((max(row_size - 1, 1),)), dma((max(row_size - 1, 1),)),
            dma((half,)), dma((half,)), dma((half,)), dma((half,)), dma((2,)),
        ],
        compiler_params=pltpu.CompilerParams(
            collective_id=0, has_side_effects=True, vmem_limit_bytes=VMEM_LIMIT
        ),
        cost_estimate=pl.CostEstimate(flops=4 * flops, bytes_accessed=30 << 20, transcendentals=0),
        name="gather_grad",
    )(out_grad, preact, weight)


def scatter_kernel(
    chips, pre_ref, weight_ref, out_ref,
    weight, rows, kept, side_out, side_in, right_out, right_in, left_out, left_in,
    weight_sem, side_send, side_recv, right_send, right_recv, left_send, left_recv,
):
    col = lax.axis_index("col")
    chip, core = lax.div(col, 2), lax.rem(col, 2)
    place = ring_position(chip, chips)
    at = lambda delta: 2 * ring_chip(place + delta, chips) + core
    right, left, side = at(1), at(-1), 2 * chip + 1 - core
    half = chips // 2
    width = weight.shape[0]
    cut = cut_of(width)
    tile = tile_of(width)
    tiles = width // tile
    block = out_ref.shape[0]

    for j in range(tiles):
        piece = pl.ds(j * tile, tile)
        pltpu.make_async_copy(weight_ref.at[piece], weight.at[piece], weight_sem.at[j]).start()
    enter((right, left, side), 1, 0)

    def remote(src, dst, peer, send, recv):
        return pltpu.make_async_remote_copy(
            src_ref=src, dst_ref=dst, send_sem=send, recv_sem=recv,
            device_id={"col": peer}, device_id_type=MESH,
        )

    def sideways(group, count):
        piece = pl.ds(0, count)
        return remote(
            side_out.at[group, piece], side_in.at[group, piece], side,
            side_send.at[group], side_recv.at[group],
        )

    def multiply(deltas, group):
        count = block * len(deltas)
        for i, delta in enumerate(deltas):
            mine = at(delta)
            other = mine + 1 - 2 * core
            rows[pl.ds(block * i, block), :] = pre_ref[
                pl.ds(pl.multiple_of(other * block, block), block), :]
            rows[pl.ds(count + block * i, block), :] = pre_ref[
                pl.ds(pl.multiple_of(mine * block, block), block), :]

        @pl.loop(0, tiles)
        def _(j):
            piece = pl.ds(pl.multiple_of(j * tile, tile), tile)
            if group == 0:
                pltpu.make_async_copy(
                    weight_ref.at[piece], weight.at[piece], weight_sem.at[j]
                ).wait()
            part = contract_cols(rows[pl.ds(0, 2 * count), :], weight[piece, :])
            side_out[group, pl.ds(0, count), piece] = part[:count].astype(jnp.bfloat16)
            kept[group, pl.ds(0, count), piece] = part[count:]

        sideways(group, count).start()
        sideways(group, count).wait_recv()

    def total(group, i, lo, size):
        piece, cols = pl.ds(block * i, block), pl.ds(lo, size)
        return kept[group, piece, cols] + side_in[group, piece, cols].astype(jnp.float32)

    def go_right(step):
        size = cut if step == 1 else width
        return remote(
            right_out.at[step - 1, :, pl.ds(0, size)], right_in.at[step - 1, :, pl.ds(0, size)],
            right, right_send.at[step - 1], right_recv.at[step - 1],
        )

    def go_left(step):
        lo, size = (cut, width - cut) if step == 1 else (0, width)
        return remote(
            left_out.at[step - 1, :, pl.ds(lo, size)], left_in.at[step - 1, :, pl.ds(lo, size)],
            left, left_send.at[step - 1], left_recv.at[step - 1],
        )

    def arrived(ref, step, lo, size):
        return ref[step - 2, :, pl.ds(lo, size)].astype(jnp.float32)

    low = lambda value: value.astype(jnp.bfloat16)
    rest = width - cut
    multiply((half,), 0)
    right_out[0, :, pl.ds(0, cut)] = low(total(0, 0, 0, cut))
    go_right(1).start()
    left_out[0, :, pl.ds(cut, rest)] = low(total(0, 0, cut, rest))
    go_left(1).start()
    for step in range(2, half + 1):
        delta = half - step + 1
        group = step - 1
        multiply((delta, -delta), group)
        go_right(step - 1).wait_recv()
        if step == 2:
            right_out[1, :, pl.ds(0, cut)] = low(
                total(1, 0, 0, cut) + arrived(right_in, 2, 0, cut))
            right_out[1, :, pl.ds(cut, rest)] = low(total(1, 0, cut, rest))
        else:
            right_out[group, :, :] = low(
                total(group, 0, 0, width) + arrived(right_in, step, 0, width))
        go_right(step).start()
        go_left(step - 1).wait_recv()
        if step == 2:
            left_out[1, :, pl.ds(0, cut)] = low(total(1, 1, 0, cut))
            left_out[1, :, pl.ds(cut, rest)] = low(
                total(1, 1, cut, rest) + arrived(left_in, 2, cut, rest))
        else:
            left_out[group, :, :] = low(
                total(group, 1, 0, width) + arrived(left_in, step, 0, width))
        go_left(step).start()
    multiply((0,), half)
    go_right(half).wait_recv()
    go_left(half).wait_recv()
    out_ref[...] = (
        total(half, 0, 0, width)
        + arrived(right_in, half + 1, 0, width)
        + arrived(left_in, half + 1, 0, width)
    )
    for step in range(1, half + 1):
        go_right(step).wait_send()
        go_left(step).wait_send()
    for group in range(half + 1):
        sideways(group, block if group in (0, half) else 2 * block).wait_send()


def multiply_and_scatter(col_size, grad_pre, weight):
    chips, half = col_size // 2, col_size // 4
    tokens, hidden = grad_pre.shape
    width = weight.shape[0]
    block = tokens // col_size
    dma = pltpu.SemaphoreType.DMA
    anywhere = pl.BlockSpec(memory_space=pl.ANY)
    vmem = pl.BlockSpec(memory_space=pltpu.VMEM)
    low, ring, group = jnp.bfloat16, (half, block, width), (half + 1, 2 * block, width)
    return pl.pallas_call(
        functools.partial(scatter_kernel, chips),
        out_shape=jax.ShapeDtypeStruct((block, width), jnp.float32),
        in_specs=[vmem, anywhere],
        out_specs=vmem,
        scratch_shapes=[
            pltpu.VMEM(weight.shape, low),
            pltpu.VMEM((4 * block, hidden), low),
            pltpu.VMEM(group, jnp.float32), pltpu.VMEM(group, low), pltpu.VMEM(group, low),
            pltpu.VMEM(ring, low), pltpu.VMEM(ring, low),
            pltpu.VMEM(ring, low), pltpu.VMEM(ring, low),
            dma((width // tile_of(width),)), dma((half + 1,)), dma((half + 1,)),
            dma((half,)), dma((half,)), dma((half,)), dma((half,)),
        ],
        compiler_params=pltpu.CompilerParams(
            collective_id=1, has_side_effects=True, vmem_limit_bytes=VMEM_LIMIT
        ),
        cost_estimate=pl.CostEstimate(
            flops=8 * tokens * hidden * width, bytes_accessed=30 << 20, transcendentals=0
        ),
        name="scatter_sums",
    )(grad_pre, weight)


def outer_kernel(factor, left_ref, right_ref, out_ref):
    out_ref[...] = (contract_rows(left_ref[...], right_ref[...]) * factor).astype(out_ref.dtype)


def scaled_outer(left, right, factor):
    tokens, width = left.shape
    hidden = right.shape[1]
    tile = tile_of(width)
    return pl.pallas_call(
        functools.partial(outer_kernel, factor),
        out_shape=jax.ShapeDtypeStruct((width, hidden), jnp.bfloat16),
        grid=(width // tile,),
        in_specs=[
            pl.BlockSpec((tokens, tile), lambda i: (0, i)),
            pl.BlockSpec((tokens, hidden), lambda i: (0, 0)),
        ],
        out_specs=pl.BlockSpec((tile, hidden), lambda i: (i, 0)),
        compiler_params=pltpu.CompilerParams(vmem_limit_bytes=40 * 1024 * 1024),
        cost_estimate=pl.CostEstimate(
            flops=2 * tokens * hidden * width, bytes_accessed=30 << 20, transcendentals=0
        ),
        name="scaled_outer",
    )(left, right)


def on_device(row_size, col_size, inputs, out_grad, preact, first_weight, second_weight):
    grad_blocks, pre_blocks, partial, partial_low = gather_and_multiply(
        row_size, col_size, out_grad, preact, second_weight
    )
    grad_whole = grad_blocks.reshape(-1, grad_blocks.shape[-1])
    pre_whole = pre_blocks.reshape(-1, pre_blocks.shape[-1]).astype(jnp.float32)
    tokens_all = grad_whole.shape[0]
    factor = 1.0 / math.sqrt(tokens_all)
    inputs, partial_low = lax.optimization_barrier((inputs, partial_low))
    input_whole = lax.all_gather(inputs, "col", axis=0, tiled=True)
    grad_act = partial
    for shift in range(1, row_size):
        turn = [(i, (i + shift) % row_size) for i in range(row_size)]
        grad_act = grad_act + lax.ppermute(partial_low, "row", turn).astype(jnp.float32)
    activated = gelu_value(pre_whole).astype(jnp.bfloat16)
    grad_second = (contract_rows(activated, grad_whole) * factor).astype(jnp.bfloat16)
    grad_pre = (grad_act * gelu_slope(pre_whole)).astype(jnp.bfloat16)
    grad_inputs = multiply_and_scatter(col_size, grad_pre, first_weight)
    grad_first = scaled_outer(input_whole, grad_pre, factor)
    return (grad_inputs, grad_first, grad_second)


def solution(mesh):
    placed = (P("col", "row"), P("col", "row"), P("row", "col"), P("row", "col"), P("col", "row"))
    return jax.shard_map(
        functools.partial(on_device, mesh.shape["row"], mesh.shape["col"]),
        mesh=mesh,
        in_specs=placed,
        out_specs=(P("col", "row"), P("row", "col"), P("col", "row")),
        check_vma=False,
    )
```

time: 397 us -> 216 us (0.54)
  waiting for transfers between devices: 280 us -> 32.9 us
  Pallas kernels: 0 us -> 139 us
  matrix products: 70.8 us -> 17.1 us
  local copies, waits for them, and re-layouts: 27.8 us -> 3.16 us
  other arithmetic: 3.14 us -> 7.71 us
    all_gather x4 -> x1, waiting for transfers between devices: 150 us -> 0.02 us  [on_device(): input_whole = lax.all_gather(inputs, 'col', axis=0, tiled=True)]
    pallas_call x0 -> x3, Pallas kernels: none -> 139 us  [the longest x1 60.9 us: gather_and_multiply(): pl.pallas_call(functools.partial(gather_kernel, row_size, chips), out_sha...]
    reduce_scatter x2 -> x0, waiting for transfers between devices: 129 us -> none  [the longest x1 70 us: on_device(): lax.psum_scatter(contract_cols(token_rows, first_weight), 'col', scatter_...]
    dot_general x2 -> x0, matrix products: 35.2 us -> none  [contract_cols(): lax.dot_general(left, right, (((1,), (1,)), ((), ())), preferred_element_...]
    ppermute x0 -> x1, waiting for transfers between devices: none -> 32.8 us  [on_device(): lax.ppermute(partial_low, 'row', turn).astype(jnp.float32)]
    unnamed x5 -> x9, local copies, waits for them, and re-layouts: 27.8 us -> 3.16 us
    dot_general x2 -> x1, matrix products: 35.6 us -> 17.1 us  [contract_rows(): lax.dot_general(left, right, (((0,), (0,)), ((), ())), preferred_element_...]
    convert_element_type x1 -> x2, other arithmetic: 3.14 us -> 7.71 us  [the longest x1 5.41 us: on_device(): grad_pre = (grad_act * gelu_slope(pre_whole)).astype(jnp.bfloat16)]
  transfers between devices with their start and end apart: 6 -> 2, of which waited for: 6 -> 1; matrix products, arithmetic and copies ran while one was open for 21% -> 12% of each run, Pallas kernels for 0% -> 28%
where the time goes in v1:
time: 216 us
  Pallas kernels  139 us (64%)
  waiting for transfers between devices  32.9 us (15%)
  matrix products  17.1 us (8%)
  between operations  14.1 us (7%)
  other arithmetic  7.71 us (4%)
  local copies, waits for them, and re-layouts  3.16 us (1%)
    pallas_call x1, Pallas kernels, gather_and_multiply(): pl.pallas_call(functools.partial(gather_kernel, row_size, chips), out_sha...  60.9 us
    pallas_call x1, Pallas kernels, multiply_and_scatter(): pl.pallas_call(functools.partial(scatter_kernel, chips), out_shape=jax.Sh...  60.6 us
    ppermute x1, waiting for transfers between devices, on_device(): lax.ppermute(partial_low, 'row', turn).astype(jnp.float32)  32.8 us
    pallas_call x1, Pallas kernels, scaled_outer(): pl.pallas_call(functools.partial(outer_kernel, factor), out_shape=jax.Sha...  17.5 us
    dot_general x1, matrix products, contract_rows(): lax.dot_general(left, right, (((0,), (0,)), ((), ())), preferred_element_...  17.1 us
    convert_element_type x1, other arithmetic, on_device(): grad_pre = (grad_act * gelu_slope(pre_whole)).astype(jnp.bfloat16)  5.41 us
  transfers between devices with their start and end apart: 2, of which 1 were waited for; matrix products, arithmetic and copies ran while one was open for 12% of the time, Pallas kernels for 28%

profile of v1, /device:TPU:0, one launch (start us, length us, event | category | flops | bytes accessed | tf_op | source)
XLA Modules:
  0.0 215.5 jit_solution(10453699003067238613)
XLA Ops:
  7.2 0.0 all-gather.2.cloned.1.call-start
  7.2 60.9 %gather_grad.1 = (bf16[16,32,4608]{2,1,0:T(8,128)(2,1)}, bf16[2,256,2304]{2,1,0:T(8,128)(2,1)}, f32[512,2304]{1,0:T(8,128)}, bf16[512,2304]{1,0:T(8,128)(2,1)}) custom-call(bf16[32,4608]{1,0:T(8,128)(2,1)} %grad_ref.1, bf16[256,2304]{1,0:T(8,128)(2,1)} %pre_ref.1, bf16[2304,4608]{1,0:T(8,128)(2,1)} %weight_ref.2), custom_call_target="tpu_custom_call" | custom-call | flops 43486543872 | bytes 31457280 | tf_op jit(solution)/shard_map/gather_grad/pallas_call | solution.py:220
  68.1 0.0 all-gather.2.cloned.1.call-update
  68.1 1.6 collective-permute-start
  69.7 2.3 %fusion.7 = bf16[2,256,2304]{2,1,0:T(8,128)(2,1)S(1)} fusion(bf16[2,256,2304]{2,1,0:T(8,128)(2,1)} %get-tuple-element.12), kind=kLoop, calls=%fused_computation.12 | loop fusion | flops 7077888 | bytes 4718592 | tf_op jit(solution)/shard_map/convert_element_type | solution.py:443
  72.0 0.0 copy-start.2
  72.0 17.1 %multiply_convert_fusion = bf16[2304,4608]{1,0:T(8,128)(2,1)} fusion(bf16[512,2304]{1,0:T(8,128)(2,1)S(1)} %bitcast.15, bf16[512,4608]{1,0:T(8,128)(2,1)} %bitcast.16), kind=kOutput, calls=%fused_computation | convolution fusion | flops 10892869632 | bytes 28311552 | tf_op jit(solution)/shard_map/dot_general | solution.py:28
  89.1 32.8 %collective-permute-done = bf16[512,2304]{1,0:T(8,128)(2,1)} collective-permute-done((bf16[512,2304]{1,0:T(8,128)(2,1)}, bf16[512,2304]{1,0:T(8,128)(2,1)}, u32[]{:S(2)}, u32[]{:S(2)}) %collective-permute-start) | collective-permute-done | bytes 2359328 | tf_op jit(solution)/shard_map/ppermute | solution.py:442
  122.0 0.0 copy-done.2
  122.0 5.4 %fusion.5.pre_ref.right_ref = bf16[512,2304]{1,0:T(8,128)(2,1)} fusion(bf16[2,256,2304]{2,1,0:T(8,128)(2,1)S(1)} %copy-done.2, f32[512,2304]{1,0:T(8,128)} %get-tuple-element.9, bf16[512,2304]{1,0:T(8,128)(2,1)} %collective-permute-done), kind=kLoop, calls=%fused_computation.7 | loop fusion | flops 15335424 | bytes 11796480 | tf_op jit(solution)/shard_map/convert_element_type | solution.py:445
  127.4 0.0 copy-start
  127.4 60.6 %scatter_sums.1 = f32[32,4608]{1,0:T(8,128)} custom-call(bf16[512,2304]{1,0:T(8,128)(2,1)} %fusion.5.pre_ref.right_ref, bf16[4608,2304]{1,0:T(8,128)(2,1)} %weight_ref.3), custom_call_target="tpu_custom_call" | custom-call | flops 43486543872 | bytes 31457280 | tf_op jit(solution)/shard_map/scatter_sums/pallas_call | solution.py:380
  188.0 0.0 all-gather.2.cloned.1.call-done.left_ref
  188.0 0.0 copy-done
  188.0 0.0 copy-start.1
  188.0 2.3 %copy-done.1 = bf16[512,4608]{1,0:T(8,128)(2,1)S(1)} copy-done((bf16[512,4608]{1,0:T(8,128)(2,1)S(1)}, bf16[512,4608]{1,0:T(8,128)(2,1)}, u32[]{:S(2)}) %copy-start.1) | copy-done | bytes 4718616
  190.3 0.0 copy-start.3
  190.3 17.5 %scaled_outer.1 = bf16[4608,2304]{1,0:T(8,128)(2,1)} custom-call(bf16[512,4608]{1,0:T(8,128)(2,1)S(1)} %copy-done.1, bf16[512,2304]{1,0:T(8,128)(2,1)S(1)} %copy-done), custom_call_target="tpu_custom_call" | custom-call | flops 10871635968 | bytes 31457280 | tf_op jit(solution)/shard_map/scaled_outer/pallas_call | solution.py:412
  207.9 0.0 copy-done.3
  207.9 0.8 copy.9
Async XLA Ops:
  7.2 180.8 %all-gather.2.cloned.1.call-start = ((), (), s32[]{:S(2)}) async-start(), calls=%async_computation | async-start | bytes 5013504 | tf_op jit(solution)/shard_map/all_gather | solution.py:438
  68.1 53.9 %collective-permute-start = (bf16[512,2304]{1,0:T(8,128)(2,1)}, bf16[512,2304]{1,0:T(8,128)(2,1)}, u32[]{:S(2)}, u32[]{:S(2)}) collective-permute-start(bf16[512,2304]{1,0:T(8,128)(2,1)} %get-tuple-element.11), channel_id=1, source_target_pairs={{0,16},{16,0},{1,17},{17,1},{2,18},{18,2},{3,19},{19,3},{4,20},{20... | collective-permute-start | bytes 7077896 | tf_op jit(solution)/shard_map/ppermute | solution.py:442
  72.0 50.0 %copy-start.2 = (bf16[2,256,2304]{2,1,0:T(8,128)(2,1)S(1)}, bf16[2,256,2304]{2,1,0:T(8,128)(2,1)}, u32[]{:S(2)}) copy-start(bf16[2,256,2304]{2,1,0:T(8,128)(2,1)} %get-tuple-element.12) | copy-start | bytes 7077892
  127.4 60.6 %copy-start = (bf16[512,2304]{1,0:T(8,128)(2,1)S(1)}, bf16[512,2304]{1,0:T(8,128)(2,1)}, u32[]{:S(2)}) copy-start(bf16[512,2304]{1,0:T(8,128)(2,1)} %fusion.5.pre_ref.right_ref) | copy-start | bytes 7077892
  188.0 2.3 %copy-start.1 = (bf16[512,4608]{1,0:T(8,128)(2,1)S(1)}, bf16[512,4608]{1,0:T(8,128)(2,1)}, u32[]{:S(2)}) copy-start(bf16[512,4608]{1,0:T(8,128)(2,1)} %all-gather.2.cloned.1.call-done.left_ref) | copy-start | bytes 14155780
  190.3 17.5 %copy-start.3 = (f32[32,4608]{1,0:T(8,128)S(1)}, f32[32,4608]{1,0:T(8,128)}, u32[]{:S(2)}) copy-start(f32[32,4608]{1,0:T(8,128)} %scatter_sums.1) | copy-start | bytes 1769476
Sparse Core Ops, SparseCore 0:
  68.2 54.8 all-gather.1

commit v2 on v1

--- a/solution.py
+++ b/solution.py
@@ -141,14 +141,16 @@
         ))
         pre_copies[-1].start()
 
-    def multiply(deltas, first):
-        count = 2 * block * len(deltas)
+    def collect(deltas):
         for i, delta in enumerate(deltas):
             origin = 2 * ring_chip(place + delta, chips)
             for k in range(2):
                 rows[pl.ds((2 * i + k) * block, block), :] = full_ref[origin + k]
 
-        @pl.loop(0, tiles)
+    def multiply(deltas, first, begin, end):
+        count = 2 * block * len(deltas)
+
+        @pl.loop(begin, end)
         def _(j):
             piece = pl.ds(pl.multiple_of(j * tile, tile), tile)
             if first:
@@ -163,10 +165,15 @@
                 out_low[pl.ds(origin, 2 * block), piece] = low[2 * block * i:2 * block * (i + 1)]
 
     slot = 1
+    early = tuple(range(2 - half, half - 1))
+    late = tuple(d for d in range(1 - half, half + 1) if d not in early)
     sideways(0, False, 0).wait_recv()
     for step in range(1, half + 1):
-        deltas = (0,) if step == 1 else (step - 1, 1 - step)
-        multiply(deltas, step == 1)
+        if step == half - 1:
+            collect(early)
+            multiply(early, True, 0, tiles // 2)
+        if step == half:
+            multiply(early, True, tiles // 2, tiles)
         from_left(step).wait_recv()
         if step < half:
             go_right(step + 1).start()
@@ -179,7 +186,8 @@
         for i, delta in enumerate(moved):
             sideways(delta, False, slot + i).wait_recv()
         slot += len(moved)
-    multiply((half,), False)
+    collect(late)
+    multiply(late, False, 0, tiles)
 
     out_copies = [
         pltpu.make_async_copy(out_sum, sum_ref, store_sem.at[0]),
@@ -229,7 +237,7 @@
         out_specs=(vmem, anywhere, anywhere, anywhere),
         scratch_shapes=[
             pltpu.VMEM(weight.shape, jnp.bfloat16),
-            pltpu.VMEM((4 * block, width), jnp.bfloat16),
+            pltpu.VMEM((tokens, width), jnp.bfloat16),
             pltpu.VMEM((tokens, hidden), jnp.float32),
             pltpu.VMEM((tokens, hidden), jnp.bfloat16),
             dma((hidden // tile_of(hidden),)), dma((2,)), dma((chips,)), dma((chips,)),
@@ -279,29 +287,45 @@
             side_send.at[group], side_recv.at[group],
         )
 
-    def multiply(deltas, group):
-        count = block * len(deltas)
-        for i, delta in enumerate(deltas):
-            mine = at(delta)
-            other = mine + 1 - 2 * core
-            rows[pl.ds(block * i, block), :] = pre_ref[
-                pl.ds(pl.multiple_of(other * block, block), block), :]
-            rows[pl.ds(count + block * i, block), :] = pre_ref[
-                pl.ds(pl.multiple_of(mine * block, block), block), :]
-
-        @pl.loop(0, tiles)
+    def members(group):
+        delta = half - group
+        return (delta,) if group in (0, half) else (delta, -delta)
+
+    def collect(groups):
+        start = 0
+        for flip in (1, 0):
+            for group in groups:
+                for delta in members(group):
+                    source = at(delta) + flip * (1 - 2 * core)
+                    rows[pl.ds(start, block), :] = pre_ref[
+                        pl.ds(pl.multiple_of(source * block, block), block), :]
+                    start += block
+
+    def multiply(groups, first, begin, end):
+        counts = [block * len(members(group)) for group in groups]
+        count = sum(counts)
+
+        @pl.loop(begin, end)
         def _(j):
             piece = pl.ds(pl.multiple_of(j * tile, tile), tile)
-            if group == 0:
+            if first:
                 pltpu.make_async_copy(
                     weight_ref.at[piece], weight.at[piece], weight_sem.at[j]
                 ).wait()
             part = contract_cols(rows[pl.ds(0, 2 * count), :], weight[piece, :])
-            side_out[group, pl.ds(0, count), piece] = part[:count].astype(jnp.bfloat16)
-            kept[group, pl.ds(0, count), piece] = part[count:]
-
-        sideways(group, count).start()
-        sideways(group, count).wait_recv()
+            start = 0
+            for group, size in zip(groups, counts):
+                side_out[group, pl.ds(0, size), piece] = part[start:start + size].astype(
+                    jnp.bfloat16)
+                kept[group, pl.ds(0, size), piece] = part[count + start:count + start + size]
+                start += size
+
+    def exchange(groups):
+        sizes = [block * len(members(group)) for group in groups]
+        for group, size in zip(groups, sizes):
+            sideways(group, size).start()
+        for group, size in zip(groups, sizes):
+            sideways(group, size).wait_recv()
 
     def total(group, i, lo, size):
         piece, cols = pl.ds(block * i, block), pl.ds(lo, size)
@@ -326,15 +350,22 @@
 
     low = lambda value: value.astype(jnp.bfloat16)
     rest = width - cut
-    multiply((half,), 0)
+    early, late = tuple(range(0, 2)), tuple(range(2, half + 1))
+    collect(early)
+    multiply(early, True, 0, tiles)
+    exchange(early)
     right_out[0, :, pl.ds(0, cut)] = low(total(0, 0, 0, cut))
     go_right(1).start()
     left_out[0, :, pl.ds(cut, rest)] = low(total(0, 0, cut, rest))
     go_left(1).start()
     for step in range(2, half + 1):
-        delta = half - step + 1
         group = step - 1
-        multiply((delta, -delta), group)
+        if step == 2:
+            collect(late)
+            multiply(late, False, 0, tiles // 2)
+        if step == 3:
+            multiply(late, False, tiles // 2, tiles)
+            exchange(late)
         go_right(step - 1).wait_recv()
         if step == 2:
             right_out[1, :, pl.ds(0, cut)] = low(
@@ -353,7 +384,6 @@
             left_out[group, :, :] = low(
                 total(group, 1, 0, width) + arrived(left_in, step, 0, width))
         go_left(step).start()
-    multiply((0,), half)
     go_right(half).wait_recv()
     go_left(half).wait_recv()
     out_ref[...] = (
@@ -384,7 +414,7 @@
         out_specs=vmem,
         scratch_shapes=[
             pltpu.VMEM(weight.shape, low),
-            pltpu.VMEM((4 * block, hidden), low),
+            pltpu.VMEM((tokens, hidden), low),
             pltpu.VMEM(group, jnp.float32), pltpu.VMEM(group, low), pltpu.VMEM(group, low),
             pltpu.VMEM(ring, low), pltpu.VMEM(ring, low),
             pltpu.VMEM(ring, low), pltpu.VMEM(ring, low),

time: 216 us -> 194 us (0.90)
  Pallas kernels: 139 us -> 118 us
    pallas_call x1, Pallas kernels: 60.6 us -> 45.9 us  [multiply_and_scatter(): pl.pallas_call(functools.partial(scatter_kernel, chips), out_shape=jax.Sh...]
    pallas_call x1, Pallas kernels: 60.9 us -> 54.7 us  [gather_and_multiply(): pl.pallas_call(functools.partial(gather_kernel, row_size, chips), out_sha...]
  transfers between devices with their start and end apart: 2 -> 2, of which waited for: 1 -> 1; matrix products, arithmetic and copies ran while one was open for 12% -> 13% of each run, Pallas kernels for 28% -> 24%
where the time goes in v2:
time: 194 us; the launch traced here: 193 us
  Pallas kernels  118 us (61%)
  waiting for transfers between devices  31.5 us (16%)
  matrix products  17.2 us (9%)
  between operations  14.1 us (7%)
  other arithmetic  7.71 us (4%)
  local copies, waits for them, and re-layouts  3.16 us (2%)
    pallas_call x1, Pallas kernels, gather_and_multiply(): pl.pallas_call(functools.partial(gather_kernel, row_size, chips), out_sha...  54.7 us
    pallas_call x1, Pallas kernels, multiply_and_scatter(): pl.pallas_call(functools.partial(scatter_kernel, chips), out_shape=jax.Sh...  45.9 us
    ppermute x1, waiting for transfers between devices, on_device(): lax.ppermute(partial_low, 'row', turn).astype(jnp.float32)  31.4 us
    pallas_call x1, Pallas kernels, scaled_outer(): pl.pallas_call(functools.partial(outer_kernel, factor), out_shape=jax.Sha...  17.5 us
    dot_general x1, matrix products, contract_rows(): lax.dot_general(left, right, (((0,), (0,)), ((), ())), preferred_element_...  17.2 us
    convert_element_type x1, other arithmetic, on_device(): grad_pre = (grad_act * gelu_slope(pre_whole)).astype(jnp.bfloat16)  5.41 us
  transfers between devices with their start and end apart: 2, of which 1 were waited for; matrix products, arithmetic and copies ran while one was open for 13% of the time, Pallas kernels for 24%

profile of v2, /device:TPU:0, one launch (start us, length us, event | category | flops | bytes accessed | tf_op | source)
XLA Modules:
  0.0 193.4 jit_solution(5117758609645332968)
XLA Ops:
  7.2 0.0 all-gather.2.cloned.1.call-start
  7.2 54.7 %gather_grad.1 = (bf16[16,32,4608]{2,1,0:T(8,128)(2,1)}, bf16[2,256,2304]{2,1,0:T(8,128)(2,1)}, f32[512,2304]{1,0:T(8,128)}, bf16[512,2304]{1,0:T(8,128)(2,1)}) custom-call(bf16[32,4608]{1,0:T(8,128)(2,1)} %grad_ref.1, bf16[256,2304]{1,0:T(8,128)(2,1)} %pre_ref.1, bf16[2304,4608]{1,0:T(8,128)(2,1)} %weight_ref.2), custom_call_target="tpu_custom_call" | custom-call | flops 43486543872 | bytes 31457280 | tf_op jit(solution)/shard_map/gather_grad/pallas_call | solution.py:228
  61.9 0.0 all-gather.2.cloned.1.call-update
  62.0 1.6 collective-permute-start
  63.5 2.3 %fusion.7 = bf16[2,256,2304]{2,1,0:T(8,128)(2,1)S(1)} fusion(bf16[2,256,2304]{2,1,0:T(8,128)(2,1)} %get-tuple-element.12), kind=kLoop, calls=%fused_computation.12 | loop fusion | flops 7077888 | bytes 4718592 | tf_op jit(solution)/shard_map/convert_element_type | solution.py:473
  65.8 0.0 copy-start.2
  65.8 17.2 %multiply_convert_fusion = bf16[2304,4608]{1,0:T(8,128)(2,1)} fusion(bf16[512,2304]{1,0:T(8,128)(2,1)S(1)} %bitcast.15, bf16[512,4608]{1,0:T(8,128)(2,1)} %bitcast.16), kind=kOutput, calls=%fused_computation | convolution fusion | flops 10892869632 | bytes 28311552 | tf_op jit(solution)/shard_map/dot_general | solution.py:28
  83.0 31.4 %collective-permute-done = bf16[512,2304]{1,0:T(8,128)(2,1)} collective-permute-done((bf16[512,2304]{1,0:T(8,128)(2,1)}, bf16[512,2304]{1,0:T(8,128)(2,1)}, u32[]{:S(2)}, u32[]{:S(2)}) %collective-permute-start) | collective-permute-done | bytes 2359328 | tf_op jit(solution)/shard_map/ppermute | solution.py:472
  114.4 0.0 copy-done.2
  114.4 5.4 %fusion.5.pre_ref.right_ref = bf16[512,2304]{1,0:T(8,128)(2,1)} fusion(bf16[2,256,2304]{2,1,0:T(8,128)(2,1)S(1)} %copy-done.2, f32[512,2304]{1,0:T(8,128)} %get-tuple-element.9, bf16[512,2304]{1,0:T(8,128)(2,1)} %collective-permute-done), kind=kLoop, calls=%fused_computation.7 | loop fusion | flops 15335424 | bytes 11796480 | tf_op jit(solution)/shard_map/convert_element_type | solution.py:475
  119.8 0.0 copy-start
  119.8 45.9 %scatter_sums.1 = f32[32,4608]{1,0:T(8,128)} custom-call(bf16[512,2304]{1,0:T(8,128)(2,1)} %fusion.5.pre_ref.right_ref, bf16[4608,2304]{1,0:T(8,128)(2,1)} %weight_ref.3), custom_call_target="tpu_custom_call" | custom-call | flops 43486543872 | bytes 31457280 | tf_op jit(solution)/shard_map/scatter_sums/pallas_call | solution.py:410
  165.8 0.0 all-gather.2.cloned.1.call-done.left_ref
  165.8 0.0 copy-done
  165.8 0.0 copy-start.1
  165.8 2.3 %copy-done.1 = bf16[512,4608]{1,0:T(8,128)(2,1)S(1)} copy-done((bf16[512,4608]{1,0:T(8,128)(2,1)S(1)}, bf16[512,4608]{1,0:T(8,128)(2,1)}, u32[]{:S(2)}) %copy-start.1) | copy-done | bytes 4718616
  168.2 0.0 copy-start.3
  168.2 17.5 %scaled_outer.1 = bf16[4608,2304]{1,0:T(8,128)(2,1)} custom-call(bf16[512,4608]{1,0:T(8,128)(2,1)S(1)} %copy-done.1, bf16[512,2304]{1,0:T(8,128)(2,1)S(1)} %copy-done), custom_call_target="tpu_custom_call" | custom-call | flops 10871635968 | bytes 31457280 | tf_op jit(solution)/shard_map/scaled_outer/pallas_call | solution.py:442
  185.7 0.0 copy-done.3
  185.7 0.8 copy.9
Async XLA Ops:
  7.2 158.7 %all-gather.2.cloned.1.call-start = ((), (), s32[]{:S(2)}) async-start(), calls=%async_computation | async-start | bytes 5013504 | tf_op jit(solution)/shard_map/all_gather | solution.py:468
  62.0 52.5 %collective-permute-start = (bf16[512,2304]{1,0:T(8,128)(2,1)}, bf16[512,2304]{1,0:T(8,128)(2,1)}, u32[]{:S(2)}, u32[]{:S(2)}) collective-permute-start(bf16[512,2304]{1,0:T(8,128)(2,1)} %get-tuple-element.11), channel_id=1, source_target_pairs={{0,16},{16,0},{1,17},{17,1},{2,18},{18,2},{3,19},{19,3},{4,20},{20... | collective-permute-start | bytes 7077896 | tf_op jit(solution)/shard_map/ppermute | solution.py:472
  65.8 48.6 %copy-start.2 = (bf16[2,256,2304]{2,1,0:T(8,128)(2,1)S(1)}, bf16[2,256,2304]{2,1,0:T(8,128)(2,1)}, u32[]{:S(2)}) copy-start(bf16[2,256,2304]{2,1,0:T(8,128)(2,1)} %get-tuple-element.12) | copy-start | bytes 7077892
  119.8 46.0 %copy-start = (bf16[512,2304]{1,0:T(8,128)(2,1)S(1)}, bf16[512,2304]{1,0:T(8,128)(2,1)}, u32[]{:S(2)}) copy-start(bf16[512,2304]{1,0:T(8,128)(2,1)} %fusion.5.pre_ref.right_ref) | copy-start | bytes 7077892
  165.8 2.3 %copy-start.1 = (bf16[512,4608]{1,0:T(8,128)(2,1)S(1)}, bf16[512,4608]{1,0:T(8,128)(2,1)}, u32[]{:S(2)}) copy-start(bf16[512,4608]{1,0:T(8,128)(2,1)} %all-gather.2.cloned.1.call-done.left_ref) | copy-start | bytes 14155780
  168.2 17.5 %copy-start.3 = (f32[32,4608]{1,0:T(8,128)S(1)}, f32[32,4608]{1,0:T(8,128)}, u32[]{:S(2)}) copy-start(f32[32,4608]{1,0:T(8,128)} %scatter_sums.1) | copy-start | bytes 1769476
Sparse Core Ops, SparseCore 0:
  62.1 52.3 all-gather.1
